TPU v7x, 32 devices: a whole 2x2x4 slice. The times are simulated.
32 devices in a mesh: groups: 2 (over y), hosts: 8 (over z, x), tensor: 2 (over core).
Axes of the slice: x: 2, y: 2, z: 4, core: 2. Of those that a mesh axis runs over, the one named last changes fastest.
Arguments:
- context_queries: bfloat16 [2048, 8192], P(('groups', 'hosts'), 'tensor'), parts along dimension 0, may hold values from -6 to 6
- context_keys: bfloat16 [2048, 1024], P(('groups', 'hosts'), 'tensor'), parts along dimension 0, may hold values from -6 to 6
- context_values: bfloat16 [2048, 1024], P(('groups', 'hosts'), 'tensor'), parts along dimension 0, may hold values from -6 to 6
- doc_ids: int32 [2048], P(('groups', 'hosts')), parts along dimension 0, may hold values from 0 to 31, never falling along the last dimension, each value on 1 to 128 neighbouring positions
- query_token_rows: bfloat16 [16, 8192], P(('groups', 'hosts'), 'tensor'), parts along dimension 0, may hold values from -6 to 6
- span_start: int32 [16], P(('groups', 'hosts')), parts along dimension 0, may hold values from 0 to 511
Outputs:
- block_out: bfloat16 [2048, 8192], P(('groups', 'hosts'), 'tensor'), parts along dimension 0
- answer: bfloat16 [16, 8192], P(('groups', 'hosts'), 'tensor'), parts along dimension 0
There are 2 independent parts, one for each index of `groups`. A program takes and returns all parts, laid end to end along the dimension named above; each array names one. Nothing has to cross between parts.
All inputs are finite; a program needn't handle non-finite values.
Results may differ from a plain program's by a relative error of at most 0.0043.
Values may be sent and summed in bfloat16 or wider, within the bound.
A program may use at most 64 MiB of HBM per device.

v0:
```python
import jax
import jax.numpy as jnp
from jax import lax
from jax.sharding import PartitionSpec as P

HEAD_SIZE = 128


MASKED_SCORE = -1e30


def from_root(value, axis, source):
    kept = jnp.where(lax.axis_index(axis) == source, value, 0).astype(value.dtype)
    return lax.psum(kept, axis)


def head_groups(matrix, kv_count):
    count_rows = matrix.shape[0]
    return matrix.reshape(
        count_rows, kv_count, matrix.shape[1] // (kv_count * HEAD_SIZE), HEAD_SIZE
    ).transpose(1, 0, 2, 3)


def kv_groups(matrix, kv_count):
    return matrix.reshape(matrix.shape[0], kv_count, HEAD_SIZE).transpose(1, 0, 2)


def block_attention(queries, key_rows, value_rows, visible, factor):
    kv_count = key_rows.shape[1] // HEAD_SIZE

    def block_per_head(operands):
        query_part, key_part, value_part = operands
        scores = (
            jnp.einsum("rgd,sd->rgs", query_part, key_part, preferred_element_type=jnp.float32)
            * factor
        )
        shown = visible[:, None, :]
        peak_score = jnp.max(jnp.where(shown, scores, MASKED_SCORE), -1, keepdims=True)
        weights = jnp.where(shown, jnp.exp(scores - peak_score), 0.0)
        totals = jnp.sum(weights, -1)
        output = jnp.einsum(
            "rgs,sd->rgd",
            weights.astype(jnp.bfloat16),
            value_part,
            preferred_element_type=jnp.float32,
        )
        return (output / totals[..., None]).astype(jnp.bfloat16)

    outputs = lax.map(
        block_per_head,
        (
            head_groups(queries, kv_count),
            kv_groups(key_rows, kv_count),
            kv_groups(value_rows, kv_count),
        ),
    )
    return outputs.transpose(1, 0, 2, 3).reshape(queries.shape[0], queries.shape[1])


def query_partials(queries, key_rows, value_rows, visible, factor):
    kv_count = key_rows.shape[1] // HEAD_SIZE

    def query_per_head(operands):
        query_part, key_part, value_part = operands
        scores = (
            jnp.einsum("qgd,sd->qgs", query_part, key_part, preferred_element_type=jnp.float32)
            * factor
        )
        shown = visible[:, None, :]
        peak_score = jnp.max(jnp.where(shown, scores, MASKED_SCORE), -1)
        weights = jnp.where(shown, jnp.exp(scores - peak_score[..., None]), 0.0)
        totals = jnp.sum(weights, -1)
        partial_acc = jnp.einsum(
            "qgs,sd->qgd",
            weights.astype(jnp.bfloat16),
            value_part,
            preferred_element_type=jnp.float32,
        )
        return (peak_score, totals, partial_acc)

    peaks, totals, accums = lax.map(
        query_per_head,
        (
            head_groups(queries, kv_count),
            kv_groups(key_rows, kv_count),
            kv_groups(value_rows, kv_count),
        ),
    )
    query_count = queries.shape[0]
    peaks = peaks.transpose(1, 0, 2).reshape(query_count, -1)
    totals = totals.transpose(1, 0, 2).reshape(query_count, -1)
    accums = accums.transpose(1, 0, 2, 3).reshape(query_count, -1)
    return (peaks, totals, accums)


def on_device(context_queries, context_keys, context_values, doc_ids, query_token_rows, span_start):
    factor = float(HEAD_SIZE) ** (-0.5)
    host_index = lax.axis_index("hosts")
    host_count = lax.axis_size("hosts")
    block_len = context_queries.shape[0]
    per_host = query_token_rows.shape[0]
    stacked = jnp.stack([context_keys, context_values])
    anchor = from_root(stacked, "hosts", 0)
    key_rows = jnp.concatenate([anchor[0], context_keys], 0)
    value_rows = jnp.concatenate([anchor[1], context_values], 0)
    positions = jnp.arange(block_len, dtype=jnp.int32)
    causal = positions[None, :] <= positions[:, None]
    own_visible = causal & (doc_ids[:, None] == doc_ids[None, :])
    front_visible = jnp.broadcast_to(host_index > 0, (block_len, block_len))
    visible = jnp.concatenate([front_visible, own_visible], 1)
    block_out = block_attention(context_queries, key_rows, value_rows, visible, factor)
    all_queries, all_spans = (
        lax.all_gather(query_token_rows, "hosts", axis=0, tiled=True),
        lax.all_gather(span_start, "hosts", axis=0, tiled=True),
    )
    key_positions = host_index * block_len + positions
    query_visible = key_positions[None, :] >= all_spans[:, None]
    peaks, totals, accums = query_partials(
        all_queries, context_keys, context_values, query_visible, factor
    )
    received = (
        lax.all_to_all(peaks, "hosts", split_axis=0, concat_axis=0, tiled=True),
        lax.all_to_all(totals, "hosts", split_axis=0, concat_axis=0, tiled=True),
        lax.all_to_all(accums, "hosts", split_axis=0, concat_axis=0, tiled=True),
    )
    source_peaks = received[0].reshape(host_count, per_host, -1)
    source_totals = received[1].reshape(host_count, per_host, -1)
    source_accums = received[2].reshape(host_count, per_host, -1)
    overall = jnp.max(source_peaks, 0)
    scales = jnp.exp(source_peaks - overall[None])
    own_totals = jnp.sum(scales * source_totals, 0)
    own_accums = jnp.sum(jnp.repeat(scales, HEAD_SIZE, axis=2) * source_accums, 0)
    answer = (own_accums / jnp.repeat(own_totals, HEAD_SIZE, axis=1)).astype(jnp.bfloat16)
    return (block_out, answer)


def solution(mesh):
    in_specs = (
        P(("groups", "hosts"), "tensor"),
        P(("groups", "hosts"), "tensor"),
        P(("groups", "hosts"), "tensor"),
        P(("groups", "hosts")),
        P(("groups", "hosts"), "tensor"),
        P(("groups", "hosts")),
    )
    out_specs = (P(("groups", "hosts"), "tensor"), P(("groups", "hosts"), "tensor"))
    return jax.shard_map(
        on_device, mesh=mesh, in_specs=in_specs, out_specs=out_specs, check_vma=False
    )
```

profile of v0, /device:TPU:0, one launch (start us, length us, event | category | flops | bytes accessed | tf_op | source)
XLA Modules:
  0.0 166.9 jit_solution(4238791645243524496)
XLA Ops:
  7.2 1.1 copy.26
  10.2 0.8 dynamic-update-slice
  11.1 13.1 %all-reduce.1 = s32[8]{0:T(128)S(1)} all-reduce(s32[8]{0:T(128)S(1)} %dynamic-update-slice), channel_id=1, replica_groups=mesh['groups'=2,'hosts'=8,'tensor'=2] {'hosts'}, use_global_device_ids=true, to_apply=%add.1 | all-reduce | flops 8 | bytes 64
  24.2 30.5 %all-gather = bf16[8,1,4096]{2,1,0:T(2,128)(2,1)S(1)} all-gather(bf16[1,1,4096]{2,1,0:T(2,128)(2,1)S(1)} %bitcast.124), channel_id=1, replica_groups=mesh['groups'=2,'hosts'=8,'tensor'=2] {'hosts'}, dimensions={0}, use_global_device_ids=true | all-gather | bytes 73728 | tf_op jit(solution)/shard_map/all_gather | solution.py:113
  55.1 2.7 %while.26 = (s32[]{:T(128)}, f32[4,8,8]{2,1,0:T(8,128)S(1)}, f32[4,8,8]{2,1,0:T(8,128)S(1)}, f32[4,8,8,128]{3,2,1,0:T(8,128)S(1)}, bf16[4,8,8,128]{3,2,0,1:T(8,1...) while((s32[]{:T(128)}, f32[4,8,8]{2,1,0:T(8,128)S(1)}, ...), condition=%wide.region_8.9_spmd.clone, body=%wide.region_5.8_spmd.clone.sunk | while | flops 4268930 | bytes 241033 | solution.py:81
  57.8 0.7 all_to_all.18
  58.5 3.3 %all-to-all-start = ((f32[8,1,32]{2,1,0:T(1,128)}), f32[8,1,32]{2,1,0:T(1,128)S(1)}, u32[]{:S(2)}, u32[]{:S(2)}) async-start(f32[8,1,32]{2,1,0:T(1,128)} %bitcast.23), calls=%async_computation | async-start | bytes 8192 | tf_op jit(solution)/shard_map/all_to_all | solution.py:122
  61.8 0.7 all_to_all.22
  62.5 5.6 %all-to-all-done = f32[8,1,32]{2,1,0:T(1,128)S(1)} async-done(((f32[8,1,32]{2,1,0:T(1,128)}), f32[8,1,32]{2,1,0:T(1,128)S(1)}, u32[]{:S(2)}, u32[]{:S(2)}) %all-to-all-start) | async-done | bytes 1056 | tf_op jit(solution)/shard_map/all_to_all | solution.py:122
  68.1 3.3 %all-to-all-start.2 = ((f32[8,1,32]{2,1,0:T(1,128)}), f32[8,1,32]{2,1,0:T(1,128)S(1)}, u32[]{:S(2)}, u32[]{:S(2)}) async-start(f32[8,1,32]{2,1,0:T(1,128)} %bitcast.30), calls=%async_computation.2 | async-start | bytes 8192 | tf_op jit(solution)/shard_map/all_to_all | solution.py:123
  71.5 0.7 maximum_select_fusion
  72.9 4.9 %all-to-all-done.2 = f32[8,1,32]{2,1,0:T(1,128)S(1)} async-done(((f32[8,1,32]{2,1,0:T(1,128)}), f32[8,1,32]{2,1,0:T(1,128)S(1)}, u32[]{:S(2)}, u32[]{:S(2)}) %all-to-all-start.2) | async-done | bytes 1056 | tf_op jit(solution)/shard_map/all_to_all | solution.py:123
  77.8 3.5 %all-to-all-start.1 = ((f32[8,1,4096]{2,1,0:T(1,128)}), f32[8,1,4096]{2,1,0:T(1,128)S(1)}, u32[]{:S(2)}, u32[]{:S(2)}) async-start(f32[8,1,4096]{2,1,0:T(1,128)} %bitcast.27), calls=%async_computation.1 | async-start | bytes 262144 | tf_op jit(solution)/shard_map/all_to_all | solution.py:124
  82.2 6.7 %all-to-all-done.1 = f32[8,1,4096]{2,1,0:T(1,128)S(1)} async-done(((f32[8,1,4096]{2,1,0:T(1,128)}), f32[8,1,4096]{2,1,0:T(1,128)S(1)}, u32[]{:S(2)}, u32[]{:S(2)}) %all-to-all-start.1) | async-done | bytes 131104 | tf_op jit(solution)/shard_map/all_to_all | solution.py:124
  89.9 58.0 %all-reduce.4.cloned.1.call-done = bf16[2,128,512]{1,2,0:T(8,128)(2,1)} async-done(((bf16[2,128,512]{1,2,0:T(8,128)(2,1)}), bf16[2,128,512]{1,2,0:T(8,128)(2,1)}) %all-reduce.4.cloned.1.call-update) | async-done | bytes 262160 | tf_op jit(solution)/shard_map/psum | solution.py:14
  147.9 1.0 fusion.52
  148.9 0.8 maximum_bitcast_fusion
  149.6 8.3 %while.25 = (s32[]{:T(128)}, bf16[4,128,8,128]{3,1,2,0:T(8,128)(2,1)S(1)}, pred[128,256]{1,0:T(8,128)(4,1)S(1)}, bf16[4,128,8,128]{1,3,2,0:T(8,128)(2,1)S(1)}, b...) while((s32[]{:T(128)}, bf16[4,128,8,128]{3,1,2,0:T(8,128)(2,1)S(1)}, ...), condition=%wide.region_4.5_spmd, body=%wide.region_1.4_spmd.sunk | while | flops 136840704 | bytes 4958285 | solution.py:49
  150.4 1.3 fusion.70
  152.5 1.3 fusion.70
  154.6 1.3 fusion.70
  156.7 1.3 fusion.70
  158.0 0.7 copy.33
  158.7 1.4 copy.53
  (64 shorter events, 9.9 us)
Async XLA Ops:
  7.2 3.7 %copy-start.2 = (bf16[128,512]{1,0:T(8,128)(2,1)S(1)}, bf16[128,512]{1,0:T(8,128)(2,1)}, u32[]{:S(2)}) copy-start(bf16[128,512]{1,0:T(8,128)(2,1)} %param.12) | copy-start | bytes 393220
  8.9 0.7 copy-start.5
  10.9 13.2 %copy-start.3 = (bf16[1,4096]{1,0:T(2,128)(2,1)S(1)}, bf16[1,4096]{1,0:T(2,128)(2,1)}, u32[]{:S(2)}) copy-start(bf16[1,4096]{1,0:T(2,128)(2,1)} %param.14) | copy-start | bytes 24580
  57.8 23.6 %copy-start = (bf16[128,4096]{1,0:T(8,128)(2,1)S(1)}, bf16[128,4096]{1,0:T(8,128)(2,1)}, u32[]{:S(2)}) copy-start(bf16[128,4096]{1,0:T(8,128)(2,1)} %param.10) | copy-start | bytes 3145732
  58.5 9.6 %all-to-all-start = ((f32[8,1,32]{2,1,0:T(1,128)}), f32[8,1,32]{2,1,0:T(1,128)S(1)}, u32[]{:S(2)}, u32[]{:S(2)}) async-start(f32[8,1,32]{2,1,0:T(1,128)} %bitcast.23), calls=%async_computation | async-start | bytes 8192 | tf_op jit(solution)/shard_map/all_to_all | solution.py:122
  68.1 9.6 %all-to-all-start.2 = ((f32[8,1,32]{2,1,0:T(1,128)}), f32[8,1,32]{2,1,0:T(1,128)S(1)}, u32[]{:S(2)}, u32[]{:S(2)}) async-start(f32[8,1,32]{2,1,0:T(1,128)} %bitcast.30), calls=%async_computation.2 | async-start | bytes 8192 | tf_op jit(solution)/shard_map/all_to_all | solution.py:123
  71.5 76.4 %all-reduce.4.cloned.1.call-start = ((), (), s32[]{:S(2)}) async-start(), calls=%async_computation.3 | async-start | bytes 524288 | tf_op jit(solution)/shard_map/psum | solution.py:14
  77.8 3.5 %copy-start.4 = (s32[128]{0:T(128)S(1)}, s32[128]{0:T(128)}, u32[]{:S(2)}) copy-start(s32[128]{0:T(128)} %param.13) | copy-start | bytes 1540
  77.8 11.1 %all-to-all-start.1 = ((f32[8,1,4096]{2,1,0:T(1,128)}), f32[8,1,4096]{2,1,0:T(1,128)S(1)}, u32[]{:S(2)}, u32[]{:S(2)}) async-start(f32[8,1,4096]{2,1,0:T(1,128)} %bitcast.27), calls=%async_computation.1 | async-start | bytes 262144 | tf_op jit(solution)/shard_map/all_to_all | solution.py:124
  82.1 67.5 %copy-start.1 = (bf16[4,128,8,128]{3,1,2,0:T(8,128)(2,1)S(1)}, bf16[4,128,8,128]{3,1,2,0:T(8,128)(2,1)}, u32[]{:S(2)}) copy-start(bf16[4,128,8,128]{3,1,2,0:T(8,128)(2,1)} %custom-call) | copy-start | bytes 3145732
Sparse Core Ops, SparseCore 0:
  75.7 72.1 all-reduce.3
where the time goes:
time: 168 us; the launch traced here: 167 us
  waiting for transfers between devices  75.3 us (45%)
  blocking collectives  43.6 us (26%)
  between operations  14.9 us (9%)
  starting transfers between devices  10.2 us (6%)
  local copies, waits for them, and re-layouts  9.16 us (5%)
  matrix products  8.18 us (5%)
  other arithmetic  5.46 us (3%)
    psum x1, waiting for transfers between devices, from_root(): return lax.psum(kept, axis)  58 us
    all_gather x1, blocking collectives, on_device(): lax.all_gather(query_token_rows, 'hosts', axis=0, tiled=True)  30.5 us
    unnamed x1, blocking collectives  13.1 us
    all_to_all x1, waiting for transfers between devices, on_device(): lax.all_to_all(accums, 'hosts', split_axis=0, concat_axis=0, tiled=True)  6.74 us
    all_to_all x1, waiting for transfers between devices, on_device(): lax.all_to_all(peaks, 'hosts', split_axis=0, concat_axis=0, tiled=True)  5.63 us
    unnamed x20, local copies, waits for them, and re-layouts  5.27 us
    dot_general x4, matrix products, block_per_head(): jnp.einsum('rgs,sd->rgd', weights.astype(jnp.bfloat16), value_part, prefe...  5.21 us
    all_to_all x1, waiting for transfers between devices, on_device(): lax.all_to_all(totals, 'hosts', split_axis=0, concat_axis=0, tiled=True)  4.86 us
  transfers between devices with their start and end apart: 4, of which 4 were waited for; matrix products, arithmetic and copies ran while one was open for 2% of the time, Pallas kernels for 0%

commit v1 on v0

v1 whole, which is shorter than its diff:
```python
import functools
import math

import jax
import jax.numpy as jnp
from jax import lax
from jax.experimental import pallas as pl
from jax.experimental.pallas import tpu as pltpu
from jax.sharding import PartitionSpec as P

HEAD_SIZE = 128
MASKED_SCORE = -1e30
SPAN_BASE = 128
MESH = pl.DeviceIdType.MESH


def each(n, body):
    if n <= 16:
        for k in range(1, n):
            body(k)
    else:
        pl.loop(1, n)(body)


def kernel(
    n, kv, group, block,
    q_hbm, k_hbm, v_hbm, docs_ref, rows_ref, span_ref,
    out_hbm, answer_ref,
    qbuf, obuf, own, anchor, bias, qrow, qall, psend, precv,
    in_sem, anc_sem, out_sem, qs_sem, qr_sem, ps_sem, pr_sem, down_sem, side_sem, ar_sem,
):
    me = lax.axis_index("hosts")
    row, col = me // 2, me % 2
    rows = n // 2
    half = kv // 2
    heads = kv * group
    width = group * HEAD_SIZE
    factor = float(HEAD_SIZE) ** -0.5 * math.log2(math.e)
    is_root = me == 0

    def load_kv(c, buf, sem):
        cols = slice(c * HEAD_SIZE, (c + 1) * HEAD_SIZE)
        return (
            pltpu.make_async_copy(k_hbm.at[:, cols], buf.at[c, 0], sem.at[c, 0]),
            pltpu.make_async_copy(v_hbm.at[:, cols], buf.at[c, 1], sem.at[c, 1]),
        )

    def load_q(c):
        return pltpu.make_async_copy(
            q_hbm.at[:, c * width:(c + 1) * width], qbuf.at[c], in_sem.at[c, 2]
        )

    @pl.when(is_root)
    def _():
        for c in range(kv):
            for copy in load_kv(c, anchor, anc_sem):
                copy.start()

    for c in range(kv):
        for copy in load_kv(c, own, in_sem):
            copy.start()
    for c in range(kv):
        load_q(c).start()

    barrier = pltpu.get_barrier_semaphore()

    def greet(k):
        pl.semaphore_signal(
            barrier, inc=1, device_id={"hosts": lax.rem(me + k, n)}, device_id_type=MESH
        )

    each(n, greet)

    for h in range(heads):
        qrow[pl.ds(h, 1), :] = rows_ref[:, h * HEAD_SIZE:(h + 1) * HEAD_SIZE].astype(jnp.float32)
    span = span_ref[0]
    qrow[heads:heads + 8, :] = jnp.full((8, HEAD_SIZE), span // SPAN_BASE, jnp.int32).astype(jnp.float32)
    qrow[heads + 8:heads + 16, :] = jnp.full((8, HEAD_SIZE), span % SPAN_BASE, jnp.int32).astype(jnp.float32)
    qall[me] = qrow[...].astype(jnp.bfloat16)

    pl.semaphore_wait(barrier, n - 1)

    def send_down(c):
        return pltpu.make_async_remote_copy(
            anchor.at[c], anchor.at[c], down_sem.at[c], ar_sem.at[c],
            device_id={"hosts": me + 2}, device_id_type=MESH,
        )

    def send_side(c):
        return pltpu.make_async_remote_copy(
            anchor.at[c], anchor.at[c], side_sem.at[c], ar_sem.at[c],
            device_id={"hosts": me + 1 - 2 * col}, device_id_type=MESH,
        )

    def arrived(c):
        pltpu.make_async_copy(anchor.at[c], anchor.at[c], ar_sem.at[c]).wait()

    @pl.when(is_root)
    def _():
        for c in range(kv):
            for copy in load_kv(c, anchor, anc_sem):
                copy.wait()
        for c in range(half):
            if rows > 1:
                send_down(c).start()
            send_side(half + c).start()
        for c in range(half):
            send_side(c).start()

    def q_copy(k):
        return pltpu.make_async_remote_copy(
            qall.at[me], qall.at[me], qs_sem.at[k], qr_sem.at[me],
            device_id={"hosts": lax.rem(me + k, n)}, device_id_type=MESH,
        )

    each(n, lambda k: q_copy(k).start())

    docs = jnp.broadcast_to(docs_ref[...].astype(jnp.float32), (block, block))
    at_row = lax.broadcasted_iota(jnp.int32, (block, block), 0)
    at_col = lax.broadcasted_iota(jnp.int32, (block, block), 1)
    shown = (at_col <= at_row) & (docs == docs.T)
    bias[...] = jnp.where(shown, 0.0, MASKED_SCORE)

    for c in range(kv):
        for copy in load_kv(c, own, in_sem):
            copy.wait()

    def from_host(k):
        return lax.rem(me + n - k, n)

    def q_arrived(k):
        source = from_host(k)
        pltpu.make_async_copy(qall.at[source], qall.at[source], qr_sem.at[source]).wait()

    each(n, q_arrived)

    def p_copy(k):
        to = lax.rem(me + k, n)
        return pltpu.make_async_remote_copy(
            psend.at[to], precv.at[me], ps_sem.at[k], pr_sem.at[me],
            device_id={"hosts": to}, device_id_type=MESH,
        )

    tokens = qall[...].astype(jnp.float32)
    spans = tokens[:, heads:heads + 8] * SPAN_BASE + tokens[:, heads + 8:heads + 16]
    place = lax.broadcasted_iota(jnp.int32, (n, 8, block), 2) + me * block
    seen = (place.astype(jnp.float32) >= spans).reshape(n * group, block)
    lane = lax.broadcasted_iota(jnp.int32, (n, group, HEAD_SIZE), 2) // 16
    stats = jnp.zeros((n, group, HEAD_SIZE), jnp.float32)
    ones = jnp.ones((block, HEAD_SIZE), jnp.bfloat16)
    for c in range(kv):
        part = tokens[:, c * group:(c + 1) * group].reshape(n * group, HEAD_SIZE)
        scores = lax.dot_general(
            part.astype(jnp.bfloat16), own[c, 0], (((1,), (1,)), ((), ())),
            preferred_element_type=jnp.float32,
        )
        scores = jnp.where(seen, scores, MASKED_SCORE)
        peak = jnp.max(scores, -1, keepdims=True)
        weights = jnp.where(seen, jnp.exp2((scores - peak) * factor), 0.0)
        acc = jnp.dot(
            weights.astype(jnp.bfloat16), jnp.concatenate([own[c, 1], ones], 1),
            preferred_element_type=jnp.float32,
        )
        psend[:, c * group:(c + 1) * group, :] = acc[:, :HEAD_SIZE].reshape(n, group, HEAD_SIZE)
        total = acc[:, HEAD_SIZE:].reshape(n, group, HEAD_SIZE)
        stats = jnp.where(lane == 2 * c, total, stats)
        peak = jnp.broadcast_to(peak, (n * group, HEAD_SIZE)).reshape(n, group, HEAD_SIZE)
        stats = jnp.where(lane == 2 * c + 1, peak, stats)
    psend[:, heads:heads + group, :] = stats
    each(n, lambda k: p_copy(k).start())
    precv[me] = psend[me]

    for j in range(half):
        c = col * half + j

        @pl.when(me > 0)
        def _():
            arrived(c)

            @pl.when(row < rows - 1)
            def _():
                send_down(c).start()

            @pl.when(row > 0)
            def _():
                send_side(c).start()

    def put(c):
        return pltpu.make_async_copy(
            obuf.at[c],
            out_hbm.at[:, pl.ds(pl.multiple_of(c * width, width), width)],
            out_sem.at[c],
        )

    for c in range(kv):
        load_q(c).wait()
    own_bias = jnp.concatenate([bias[...], bias[...]], 0)
    wide_ones = jnp.ones((2 * block, HEAD_SIZE), jnp.bfloat16)

    @pl.loop(0, kv)
    def _(j):
        c = lax.rem(col * half + j, kv)

        @pl.when((me > 0) & (j >= half))
        def _():
            arrived(c)

        keys = jnp.concatenate([anchor[c, 0], own[c, 0]], 0)
        values = jnp.concatenate([anchor[c, 1], own[c, 1]], 0)
        values = jnp.concatenate([values, wide_ones], 1)
        for g in range(0, group, 2):
            queries = jnp.concatenate(
                [qbuf[c, :, (g + i) * HEAD_SIZE:(g + i + 1) * HEAD_SIZE] for i in range(2)], 0
            )
            scores = lax.dot_general(
                queries, keys, (((1,), (1,)), ((), ())), preferred_element_type=jnp.float32
            )
            front = jnp.where(is_root, MASKED_SCORE, scores[:, :block])
            back = scores[:, block:] + own_bias
            top = jnp.max(jnp.maximum(front, back), -1, keepdims=True)
            weights = jnp.concatenate(
                [jnp.exp2((front - top) * factor), jnp.exp2((back - top) * factor)], 1
            ).astype(jnp.bfloat16)
            acc = jnp.dot(weights, values, preferred_element_type=jnp.float32)
            result = (acc[:, :HEAD_SIZE] / acc[:, HEAD_SIZE:]).astype(jnp.bfloat16)
            for i in range(2):
                obuf[c, :, (g + i) * HEAD_SIZE:(g + i + 1) * HEAD_SIZE] = result[i * block:(i + 1) * block]
        put(c).start()

    def p_arrived(k):
        source = from_host(k)
        pltpu.make_async_copy(precv.at[source], precv.at[source], pr_sem.at[source]).wait()

    each(n, p_arrived)
    stats = precv[:, heads:heads + group, :]
    for c in range(kv):
        total = stats[:, :, 32 * c:32 * c + 1]
        peak = stats[:, :, 32 * c + 16:32 * c + 17]
        scale = jnp.exp2((peak - jnp.max(peak, 0, keepdims=True)) * factor)
        total = jnp.sum(scale * total, 0)
        merged = jnp.sum(scale * precv[:, c * group:(c + 1) * group, :], 0)
        answer_ref[c * group:(c + 1) * group, :] = merged / total

    each(n, lambda k: q_copy(k).wait_send())
    each(n, lambda k: p_copy(k).wait_send())

    @pl.when(is_root)
    def _():
        for c in range(half):
            if rows > 1:
                send_down(c).wait_send()
            send_side(half + c).wait_send()
        for c in range(half):
            send_side(c).wait_send()

    for j in range(half):
        c = col * half + j

        @pl.when((me > 0) & (row < rows - 1))
        def _():
            send_down(c).wait_send()

        @pl.when(row > 0)
        def _():
            send_side(c).wait_send()

    for c in range(kv):
        put(c).wait()


def on_device(n, context_queries, context_keys, context_values, doc_ids, query_token_rows, span_start):
    block = context_queries.shape[0]
    kv = context_keys.shape[1] // HEAD_SIZE
    group = context_queries.shape[1] // context_keys.shape[1]
    heads = kv * group
    width = group * HEAD_SIZE
    any_spec = pl.BlockSpec(memory_space=pl.ANY)
    vmem_spec = pl.BlockSpec(memory_space=pltpu.VMEM)
    dma = pltpu.SemaphoreType.DMA
    block_out, answer = pl.pallas_call(
        functools.partial(kernel, n, kv, group, block),
        out_shape=(
            jax.ShapeDtypeStruct(context_queries.shape, jnp.bfloat16),
            jax.ShapeDtypeStruct((heads, HEAD_SIZE), jnp.float32),
        ),
        in_specs=[any_spec, any_spec, any_spec, vmem_spec, vmem_spec, pl.BlockSpec(memory_space=pltpu.SMEM)],
        out_specs=(any_spec, vmem_spec),
        scratch_shapes=[
            pltpu.VMEM((kv, block, width), jnp.bfloat16),
            pltpu.VMEM((kv, block, width), jnp.bfloat16),
            pltpu.VMEM((kv, 2, block, HEAD_SIZE), jnp.bfloat16),
            pltpu.VMEM((kv, 2, block, HEAD_SIZE), jnp.bfloat16),
            pltpu.VMEM((block, block), jnp.float32),
            pltpu.VMEM((heads + 16, HEAD_SIZE), jnp.float32),
            pltpu.VMEM((n, heads + 16, HEAD_SIZE), jnp.bfloat16),
            pltpu.VMEM((n, heads + 8, HEAD_SIZE), jnp.float32),
            pltpu.VMEM((n, heads + 8, HEAD_SIZE), jnp.float32),
            dma((kv, 3)), dma((kv, 2)), dma((kv,)),
            dma((n,)), dma((n,)), dma((n,)), dma((n,)),
            dma((kv,)), dma((kv,)), dma((kv,)),
        ],
        compiler_params=pltpu.CompilerParams(
            collective_id=0, has_side_effects=True, vmem_limit_bytes=40 * 1024 * 1024
        ),
    )(
        context_queries, context_keys, context_values,
        doc_ids.reshape(1, block), query_token_rows, span_start,
    )
    return block_out, answer.reshape(1, heads * HEAD_SIZE).astype(jnp.bfloat16)


def solution(mesh):
    in_specs = (
        P(("groups", "hosts"), "tensor"),
        P(("groups", "hosts"), "tensor"),
        P(("groups", "hosts"), "tensor"),
        P(("groups", "hosts")),
        P(("groups", "hosts"), "tensor"),
        P(("groups", "hosts")),
    )
    out_specs = (P(("groups", "hosts"), "tensor"), P(("groups", "hosts"), "tensor"))
    return jax.shard_map(
        functools.partial(on_device, mesh.shape["hosts"]),
        mesh=mesh, in_specs=in_specs, out_specs=out_specs, check_vma=False,
    )
```

time: 168 us -> 37.8 us (0.22)
  the two profiles are of different devices: /device:TPU:0 before, /device:TPU:28 now
where the time goes in v1:
time: 37.8 us; the launch traced here: 37.6 us
  Pallas kernels  30.3 us (80%)
  local copies, waits for them, and re-layouts  5.98 us (16%)
  between operations  1.31 us (3%)
    pallas_call x1, Pallas kernels, on_device(): pl.pallas_call(functools.partial(kernel, n, kv, group, block), out_shape=...  30.3 us
    unnamed x12, local copies, waits for them, and re-layouts  5.98 us

profile of v1, /device:TPU:28, one launch (start us, length us, event | category | flops | bytes accessed | tf_op | source)
XLA Modules:
  0.0 37.6 jit_solution(4346318635511766862)
XLA Ops:
  1.3 0.0 copy-start.4
  1.3 0.6 %copy-done.4 = s32[128]{0:T(128)S(1)} copy-done((s32[128]{0:T(128)S(1)}, s32[128]{0:T(128)}, u32[]{:S(2)}) %copy-start.4) | copy-done | bytes 536
  1.9 0.0 copy-start
  1.9 1.2 %copy-done = bf16[128,4096]{1,0:T(8,128)(2,1)S(1)} copy-done((bf16[128,4096]{1,0:T(8,128)(2,1)S(1)}, bf16[128,4096]{1,0:T(8,128)(2,1)}, u32[]{:S(2)}) %copy-start) | copy-done | bytes 1048600
  3.2 0.0 copy-start.1
  3.2 0.9 %copy-done.1 = bf16[128,512]{1,0:T(8,128)(2,1)S(1)} copy-done((bf16[128,512]{1,0:T(8,128)(2,1)S(1)}, bf16[128,512]{1,0:T(8,128)(2,1)}, u32[]{:S(2)}) %copy-start.1) | copy-done | bytes 131096
  4.1 0.0 copy-start.2
  4.1 0.9 %copy-done.2 = bf16[128,512]{1,0:T(8,128)(2,1)S(1)} copy-done((bf16[128,512]{1,0:T(8,128)(2,1)S(1)}, bf16[128,512]{1,0:T(8,128)(2,1)}, u32[]{:S(2)}) %copy-start.2) | copy-done | bytes 131096
  5.0 0.0 copy-start.3
  5.0 0.7 %copy-done.3 = bf16[1,4096]{1,0:T(2,128)(2,1)S(1)} copy-done((bf16[1,4096]{1,0:T(2,128)(2,1)S(1)}, bf16[1,4096]{1,0:T(2,128)(2,1)}, u32[]{:S(2)}) %copy-start.3) | copy-done | bytes 8216
  5.7 30.3 %shard_map.77 = (bf16[128,4096]{1,0:T(8,128)(2,1)S(1)}, f32[32,128]{1,0:T(8,128)S(1)}) custom-call(bf16[128,4096]{1,0:T(8,128)(2,1)S(1)} %copy-done, bf16[128,512]{1,0:T(8,128)(2,1)S(1)} %copy-done.1, bf16[128,512]{1,0:T(8,128)(2,1)S(1)} %copy-done.2, s32[1,128]{1,0:T(1,128)S(1)} %bitcast.7, bf16[1,4096]{1,0:T(2,128)(2,1)S(1)} %copy-done.3, s32[1]{0:T(128)S(6)} %copy.12.span_ref), custom_call_target="tpu_custom_call" | custom-call | tf_op jit(solution)/shard_map/pallas_call | solution.py:280
  36.0 0.6 %copy.10 = bf16[1,1,32,128]{3,1,2,0:T(2,128)(2,1)} copy(bf16[1,1,32,128]{3,2,1,0:T(8,128)(2,1)S(1)} %convert_bitcast_fusion) | data formatting | bytes 16384
  36.6 1.0 %copy.13 = bf16[128,4096]{1,0:T(8,128)(2,1)} copy(bf16[128,4096]{1,0:T(8,128)(2,1)S(1)} %get-tuple-element.8) | data formatting | bytes 2097152
  (1 shorter events, 0.0 us)
Async XLA Ops:
  1.3 0.7 %copy-start.4 = (s32[128]{0:T(128)S(1)}, s32[128]{0:T(128)}, u32[]{:S(2)}) copy-start(s32[128]{0:T(128)} %param.9) | copy-start | bytes 1540
  1.9 1.2 %copy-start = (bf16[128,4096]{1,0:T(8,128)(2,1)S(1)}, bf16[128,4096]{1,0:T(8,128)(2,1)}, u32[]{:S(2)}) copy-start(bf16[128,4096]{1,0:T(8,128)(2,1)} %q_hbm.1) | copy-start | bytes 3145732
  3.2 0.9 %copy-start.1 = (bf16[128,512]{1,0:T(8,128)(2,1)S(1)}, bf16[128,512]{1,0:T(8,128)(2,1)}, u32[]{:S(2)}) copy-start(bf16[128,512]{1,0:T(8,128)(2,1)} %k_hbm.1) | copy-start | bytes 393220
  4.1 0.9 %copy-start.2 = (bf16[128,512]{1,0:T(8,128)(2,1)S(1)}, bf16[128,512]{1,0:T(8,128)(2,1)}, u32[]{:S(2)}) copy-start(bf16[128,512]{1,0:T(8,128)(2,1)} %v_hbm.1) | copy-start | bytes 393220
  5.0 0.7 %copy-start.3 = (bf16[1,4096]{1,0:T(2,128)(2,1)S(1)}, bf16[1,4096]{1,0:T(2,128)(2,1)}, u32[]{:S(2)}) copy-start(bf16[1,4096]{1,0:T(2,128)(2,1)} %rows_ref.1) | copy-start | bytes 24580

commit v2 on v1

--- a/solution.py
+++ b/solution.py
@@ -24,15 +24,15 @@
 
 def kernel(
     n, kv, group, block,
-    q_hbm, k_hbm, v_hbm, docs_ref, rows_ref, span_ref,
+    q_hbm, k_hbm, v_hbm, docs_hbm, rows_hbm, span_ref,
     out_hbm, answer_ref,
-    qbuf, obuf, own, anchor, bias, qrow, qall, psend, precv,
-    in_sem, anc_sem, out_sem, qs_sem, qr_sem, ps_sem, pr_sem, down_sem, side_sem, ar_sem,
+    docs_ref, rows_ref, qbuf, obuf, own, anchor, bias, qrow, qall, psend, precv,
+    in_sem, anc_sem, out_sem, small_sem, qs_sem, qr_sem, ps_sem, pr_sem, scatter_sem, pass_sem, ar_sem,
 ):
     me = lax.axis_index("hosts")
-    row, col = me // 2, me % 2
-    rows = n // 2
-    half = kv // 2
+    pieces = 2 * kv
+    spread = n // pieces
+    mine = me // spread
     heads = kv * group
     width = group * HEAD_SIZE
     factor = float(HEAD_SIZE) ** -0.5 * math.log2(math.e)
@@ -50,6 +50,13 @@
             q_hbm.at[:, c * width:(c + 1) * width], qbuf.at[c], in_sem.at[c, 2]
         )
 
+    small = (
+        pltpu.make_async_copy(rows_hbm, rows_ref, small_sem.at[0]),
+        pltpu.make_async_copy(docs_hbm, docs_ref, small_sem.at[1]),
+    )
+    for copy in small:
+        copy.start()
+
     @pl.when(is_root)
     def _():
         for c in range(kv):
@@ -70,6 +77,9 @@
         )
 
     each(n, greet)
+
+    for copy in small:
+        copy.wait()
 
     for h in range(heads):
         qrow[pl.ds(h, 1), :] = rows_ref[:, h * HEAD_SIZE:(h + 1) * HEAD_SIZE].astype(jnp.float32)
@@ -80,32 +90,37 @@
 
     pl.semaphore_wait(barrier, n - 1)
 
-    def send_down(c):
+    def scatter(p):
+        piece = anchor.at[p // 2, p % 2]
         return pltpu.make_async_remote_copy(
-            anchor.at[c], anchor.at[c], down_sem.at[c], ar_sem.at[c],
-            device_id={"hosts": me + 2}, device_id_type=MESH,
-        )
-
-    def send_side(c):
+            piece, piece, scatter_sem.at[p], ar_sem.at[p],
+            device_id={"hosts": jnp.int32(p * spread)}, device_id_type=MESH,
+        )
+
+    def pass_on(k):
+        piece = anchor.at[mine // 2, mine % 2]
         return pltpu.make_async_remote_copy(
-            anchor.at[c], anchor.at[c], side_sem.at[c], ar_sem.at[c],
-            device_id={"hosts": me + 1 - 2 * col}, device_id_type=MESH,
-        )
-
-    def arrived(c):
-        pltpu.make_async_copy(anchor.at[c], anchor.at[c], ar_sem.at[c]).wait()
+            piece, piece, pass_sem.at[k], ar_sem.at[mine],
+            device_id={"hosts": lax.rem(me + k, n)}, device_id_type=MESH,
+        )
+
+    def arrived(p):
+        piece = anchor.at[p // 2, p % 2]
+        pltpu.make_async_copy(piece, piece, ar_sem.at[p]).wait()
+
+    def when_not_root(k, act):
+        @pl.when(lax.rem(me + k, n) > 0)
+        def _():
+            act(pass_on(k))
 
     @pl.when(is_root)
     def _():
         for c in range(kv):
             for copy in load_kv(c, anchor, anc_sem):
                 copy.wait()
-        for c in range(half):
-            if rows > 1:
-                send_down(c).start()
-            send_side(half + c).start()
-        for c in range(half):
-            send_side(c).start()
+        for p in reversed(range(1, pieces)):
+            scatter(p).start()
+        each(n, lambda k: pass_on(k).start())
 
     def q_copy(k):
         return pltpu.make_async_remote_copy(
@@ -114,6 +129,13 @@
         )
 
     each(n, lambda k: q_copy(k).start())
+
+    is_owner = (lax.rem(me, spread) == 0) & (me > 0)
+
+    @pl.when(is_owner)
+    def _():
+        arrived(mine)
+        each(n, lambda k: when_not_root(k, lambda copy: copy.start()))
 
     docs = jnp.broadcast_to(docs_ref[...].astype(jnp.float32), (block, block))
     at_row = lax.broadcasted_iota(jnp.int32, (block, block), 0)
@@ -170,21 +192,6 @@
     each(n, lambda k: p_copy(k).start())
     precv[me] = psend[me]
 
-    for j in range(half):
-        c = col * half + j
-
-        @pl.when(me > 0)
-        def _():
-            arrived(c)
-
-            @pl.when(row < rows - 1)
-            def _():
-                send_down(c).start()
-
-            @pl.when(row > 0)
-            def _():
-                send_side(c).start()
-
     def put(c):
         return pltpu.make_async_copy(
             obuf.at[c],
@@ -199,11 +206,12 @@
 
     @pl.loop(0, kv)
     def _(j):
-        c = lax.rem(col * half + j, kv)
-
-        @pl.when((me > 0) & (j >= half))
-        def _():
-            arrived(c)
+        c = lax.rem(mine // 2 + j, kv)
+        for i in range(2):
+
+            @pl.when((me > 0) & ~(is_owner & (2 * c + i == mine)))
+            def _():
+                arrived(2 * c + i)
 
         keys = jnp.concatenate([anchor[c, 0], own[c, 0]], 0)
         values = jnp.concatenate([anchor[c, 1], own[c, 1]], 0)
@@ -246,23 +254,13 @@
 
     @pl.when(is_root)
     def _():
-        for c in range(half):
-            if rows > 1:
-                send_down(c).wait_send()
-            send_side(half + c).wait_send()
-        for c in range(half):
-            send_side(c).wait_send()
-
-    for j in range(half):
-        c = col * half + j
-
-        @pl.when((me > 0) & (row < rows - 1))
-        def _():
-            send_down(c).wait_send()
-
-        @pl.when(row > 0)
-        def _():
-            send_side(c).wait_send()
+        for p in range(1, pieces):
+            scatter(p).wait_send()
+        each(n, lambda k: pass_on(k).wait_send())
+
+    @pl.when(is_owner)
+    def _():
+        each(n, lambda k: when_not_root(k, lambda copy: copy.wait_send()))
 
     for c in range(kv):
         put(c).wait()
@@ -275,6 +273,7 @@
     heads = kv * group
     width = group * HEAD_SIZE
     any_spec = pl.BlockSpec(memory_space=pl.ANY)
+    hbm_spec = pl.BlockSpec(memory_space=pltpu.HBM)
     vmem_spec = pl.BlockSpec(memory_space=pltpu.VMEM)
     dma = pltpu.SemaphoreType.DMA
     block_out, answer = pl.pallas_call(
@@ -283,9 +282,11 @@
             jax.ShapeDtypeStruct(context_queries.shape, jnp.bfloat16),
             jax.ShapeDtypeStruct((heads, HEAD_SIZE), jnp.float32),
         ),
-        in_specs=[any_spec, any_spec, any_spec, vmem_spec, vmem_spec, pl.BlockSpec(memory_space=pltpu.SMEM)],
+        in_specs=[hbm_spec] * 5 + [pl.BlockSpec(memory_space=pltpu.SMEM)],
         out_specs=(any_spec, vmem_spec),
         scratch_shapes=[
+            pltpu.VMEM((1, block), jnp.int32),
+            pltpu.VMEM(query_token_rows.shape, jnp.bfloat16),
             pltpu.VMEM((kv, block, width), jnp.bfloat16),
             pltpu.VMEM((kv, block, width), jnp.bfloat16),
             pltpu.VMEM((kv, 2, block, HEAD_SIZE), jnp.bfloat16),
@@ -295,9 +296,9 @@
             pltpu.VMEM((n, heads + 16, HEAD_SIZE), jnp.bfloat16),
             pltpu.VMEM((n, heads + 8, HEAD_SIZE), jnp.float32),
             pltpu.VMEM((n, heads + 8, HEAD_SIZE), jnp.float32),
-            dma((kv, 3)), dma((kv, 2)), dma((kv,)),
+            dma((kv, 3)), dma((kv, 2)), dma((kv,)), dma((2,)),
             dma((n,)), dma((n,)), dma((n,)), dma((n,)),
-            dma((kv,)), dma((kv,)), dma((kv,)),
+            dma((2 * kv,)), dma((n,)), dma((2 * kv,)),
         ],
         compiler_params=pltpu.CompilerParams(
             collective_id=0, has_side_effects=True, vmem_limit_bytes=40 * 1024 * 1024

time: 37.8 us -> 33.9 us (0.90)
  the two profiles are of different devices: /device:TPU:28 before, /device:TPU:0 now
where the time goes in v2:
time: 33.9 us; the launch traced here: 33.6 us
  Pallas kernels  26.3 us (78%)
  local copies, waits for them, and re-layouts  5.98 us (18%)
  between operations  1.31 us (4%)
    pallas_call x1, Pallas kernels, on_device(): pl.pallas_call(functools.partial(kernel, n, kv, group, block), out_shape=...  26.3 us
    unnamed x12, local copies, waits for them, and re-layouts  5.98 us

profile of v2, /device:TPU:0, one launch (start us, length us, event | category | flops | bytes accessed | tf_op | source)
XLA Modules:
  0.0 33.6 jit_solution(8968992300049229076)
XLA Ops:
  1.3 0.0 copy-start.4
  1.3 0.6 %copy-done.4 = s32[128]{0:T(128)S(1)} copy-done((s32[128]{0:T(128)S(1)}, s32[128]{0:T(128)}, u32[]{:S(2)}) %copy-start.4) | copy-done | bytes 536
  1.9 0.0 copy-start
  1.9 1.2 %copy-done = bf16[128,4096]{1,0:T(8,128)(2,1)S(1)} copy-done((bf16[128,4096]{1,0:T(8,128)(2,1)S(1)}, bf16[128,4096]{1,0:T(8,128)(2,1)}, u32[]{:S(2)}) %copy-start) | copy-done | bytes 1048600
  3.2 0.0 copy-start.1
  3.2 0.9 %copy-done.1 = bf16[128,512]{1,0:T(8,128)(2,1)S(1)} copy-done((bf16[128,512]{1,0:T(8,128)(2,1)S(1)}, bf16[128,512]{1,0:T(8,128)(2,1)}, u32[]{:S(2)}) %copy-start.1) | copy-done | bytes 131096
  4.1 0.0 copy-start.2
  4.1 0.9 %copy-done.2 = bf16[128,512]{1,0:T(8,128)(2,1)S(1)} copy-done((bf16[128,512]{1,0:T(8,128)(2,1)S(1)}, bf16[128,512]{1,0:T(8,128)(2,1)}, u32[]{:S(2)}) %copy-start.2) | copy-done | bytes 131096
  5.0 0.0 copy-start.3
  5.0 0.7 %copy-done.3 = bf16[1,4096]{1,0:T(2,128)(2,1)S(1)} copy-done((bf16[1,4096]{1,0:T(2,128)(2,1)S(1)}, bf16[1,4096]{1,0:T(2,128)(2,1)}, u32[]{:S(2)}) %copy-start.3) | copy-done | bytes 8216
  5.7 26.3 %shard_map.77 = (bf16[128,4096]{1,0:T(8,128)(2,1)S(1)}, f32[32,128]{1,0:T(8,128)S(1)}) custom-call(bf16[128,4096]{1,0:T(8,128)(2,1)S(1)} %copy-done, bf16[128,512]{1,0:T(8,128)(2,1)S(1)} %copy-done.1, bf16[128,512]{1,0:T(8,128)(2,1)S(1)} %copy-done.2, s32[1,128]{1,0:T(1,128)S(1)} %bitcast.7, bf16[1,4096]{1,0:T(2,128)(2,1)S(1)} %copy-done.3, s32[1]{0:T(128)S(6)} %copy.12.span_ref), custom_call_target="tpu_custom_call" | custom-call | tf_op jit(solution)/shard_map/pallas_call | solution.py:279
  32.0 0.6 %copy.10 = bf16[1,1,32,128]{3,1,2,0:T(2,128)(2,1)} copy(bf16[1,1,32,128]{3,2,1,0:T(8,128)(2,1)S(1)} %convert_bitcast_fusion) | data formatting | bytes 16384
  32.6 1.0 %copy.13 = bf16[128,4096]{1,0:T(8,128)(2,1)} copy(bf16[128,4096]{1,0:T(8,128)(2,1)S(1)} %get-tuple-element.8) | data formatting | bytes 2097152
  (1 shorter events, 0.0 us)
Async XLA Ops:
  1.3 0.7 %copy-start.4 = (s32[128]{0:T(128)S(1)}, s32[128]{0:T(128)}, u32[]{:S(2)}) copy-start(s32[128]{0:T(128)} %param.9) | copy-start | bytes 1540
  1.9 1.2 %copy-start = (bf16[128,4096]{1,0:T(8,128)(2,1)S(1)}, bf16[128,4096]{1,0:T(8,128)(2,1)}, u32[]{:S(2)}) copy-start(bf16[128,4096]{1,0:T(8,128)(2,1)} %q_hbm.1) | copy-start | bytes 3145732
  3.2 0.9 %copy-start.1 = (bf16[128,512]{1,0:T(8,128)(2,1)S(1)}, bf16[128,512]{1,0:T(8,128)(2,1)}, u32[]{:S(2)}) copy-start(bf16[128,512]{1,0:T(8,128)(2,1)} %k_hbm.1) | copy-start | bytes 393220
  4.1 0.9 %copy-start.2 = (bf16[128,512]{1,0:T(8,128)(2,1)S(1)}, bf16[128,512]{1,0:T(8,128)(2,1)}, u32[]{:S(2)}) copy-start(bf16[128,512]{1,0:T(8,128)(2,1)} %v_hbm.1) | copy-start | bytes 393220
  5.0 0.7 %copy-start.3 = (bf16[1,4096]{1,0:T(2,128)(2,1)S(1)}, bf16[1,4096]{1,0:T(2,128)(2,1)}, u32[]{:S(2)}) copy-start(bf16[1,4096]{1,0:T(2,128)(2,1)} %rows_hbm.1) | copy-start | bytes 24580

commit v3 on v2

--- a/solution.py
+++ b/solution.py
@@ -304,8 +304,14 @@
             collective_id=0, has_side_effects=True, vmem_limit_bytes=40 * 1024 * 1024
         ),
     )(
-        context_queries, context_keys, context_values,
-        doc_ids.reshape(1, block), query_token_rows, span_start,
+        *[
+            pltpu.with_memory_space_constraint(array, pltpu.HBM)
+            for array in (
+                context_queries, context_keys, context_values,
+                doc_ids.reshape(1, block), query_token_rows,
+            )
+        ],
+        span_start,
     )
     return block_out, answer.reshape(1, heads * HEAD_SIZE).astype(jnp.bfloat16)
 

time: 33.9 us -> 29.3 us (0.86)
  local copies, waits for them, and re-layouts: 5.98 us -> 1.59 us
    unnamed x12 -> x2, local copies, waits for them, and re-layouts: 5.98 us -> 1.59 us
where the time goes in v3:
time: 29.3 us; the launch traced here: 29.1 us
  Pallas kernels  26.2 us (89%)
  local copies, waits for them, and re-layouts  1.59 us (5%)
  between operations  1.29 us (4%)
    pallas_call x1, Pallas kernels, on_device(): pl.pallas_call(functools.partial(kernel, n, kv, group, block), out_shape=...  26.2 us
    unnamed x2, local copies, waits for them, and re-layouts  1.59 us

profile of v3, /device:TPU:0, one launch (start us, length us, event | category | flops | bytes accessed | tf_op | source)
XLA Modules:
  0.0 29.1 jit_solution(1463952298945493734)
XLA Ops:
  1.3 26.2 %shard_map.77 = (bf16[128,4096]{1,0:T(8,128)(2,1)S(1)}, f32[32,128]{1,0:T(8,128)S(1)}) custom-call(bf16[128,4096]{1,0:T(8,128)(2,1)} %q_hbm.1, bf16[128,512]{1,0:T(8,128)(2,1)} %k_hbm.1, bf16[128,512]{1,0:T(8,128)(2,1)} %v_hbm.1, s32[1,128]{1,0:T(1,128)} %bitcast.8, bf16[1,4096]{1,0:T(2,128)(2,1)} %rows_hbm.1, s32[1]{0:T(128)S(6)} %copy.12.span_ref), custom_call_target="tpu_custom_call" | custom-call | tf_op jit(solution)/shard_map/pallas_call | solution.py:279
  27.5 0.6 %copy.10 = bf16[1,1,32,128]{3,1,2,0:T(2,128)(2,1)} copy(bf16[1,1,32,128]{3,2,1,0:T(8,128)(2,1)S(1)} %convert_bitcast_fusion) | data formatting | bytes 16384
  28.1 1.0 %copy.13 = bf16[128,4096]{1,0:T(8,128)(2,1)} copy(bf16[128,4096]{1,0:T(8,128)(2,1)S(1)} %get-tuple-element.8) | data formatting | bytes 2097152
  (1 shorter events, 0.0 us)

commit v4 on v3

--- a/solution.py
+++ b/solution.py
@@ -26,13 +26,18 @@
     n, kv, group, block,
     q_hbm, k_hbm, v_hbm, docs_hbm, rows_hbm, span_ref,
     out_hbm, answer_ref,
-    docs_ref, rows_ref, qbuf, obuf, own, anchor, bias, qrow, qall, psend, precv,
+    docs_ref, rows_ref, qbuf, obuf, own, anchor, bias, qrow, qall, pwide, psend, precv,
     in_sem, anc_sem, out_sem, small_sem, qs_sem, qr_sem, ps_sem, pr_sem, scatter_sem, pass_sem, ar_sem,
 ):
     me = lax.axis_index("hosts")
-    pieces = 2 * kv
-    spread = n // pieces
-    mine = me // spread
+    length = 2 * kv * block
+    owners = min(n - 1, 7)
+    size = length // owners // 16 * 16
+    extra = length - owners * size
+    pieces = [
+        (1 + i * ((n - 1) // owners), i * size + (extra if i else 0), size + (0 if i else extra))
+        for i in range(owners)
+    ]
     heads = kv * group
     width = group * HEAD_SIZE
     factor = float(HEAD_SIZE) ** -0.5 * math.log2(math.e)
@@ -40,9 +45,10 @@
 
     def load_kv(c, buf, sem):
         cols = slice(c * HEAD_SIZE, (c + 1) * HEAD_SIZE)
+        at = 2 * c * block
         return (
-            pltpu.make_async_copy(k_hbm.at[:, cols], buf.at[c, 0], sem.at[c, 0]),
-            pltpu.make_async_copy(v_hbm.at[:, cols], buf.at[c, 1], sem.at[c, 1]),
+            pltpu.make_async_copy(k_hbm.at[:, cols], buf.at[pl.ds(at, block)], sem.at[c, 0]),
+            pltpu.make_async_copy(v_hbm.at[:, cols], buf.at[pl.ds(at + block, block)], sem.at[c, 1]),
         )
 
     def load_q(c):
@@ -90,37 +96,39 @@
 
     pl.semaphore_wait(barrier, n - 1)
 
-    def scatter(p):
-        piece = anchor.at[p // 2, p % 2]
+    def scatter(i):
+        host, start, count = pieces[i]
+        piece = anchor.at[pl.ds(start, count)]
         return pltpu.make_async_remote_copy(
-            piece, piece, scatter_sem.at[p], ar_sem.at[p],
-            device_id={"hosts": jnp.int32(p * spread)}, device_id_type=MESH,
-        )
-
-    def pass_on(k):
-        piece = anchor.at[mine // 2, mine % 2]
+            piece, piece, scatter_sem.at[i], ar_sem.at[i],
+            device_id={"hosts": jnp.int32(host)}, device_id_type=MESH,
+        )
+
+    def pass_on(i, k):
+        host, start, count = pieces[i]
+        piece = anchor.at[pl.ds(start, count)]
         return pltpu.make_async_remote_copy(
-            piece, piece, pass_sem.at[k], ar_sem.at[mine],
+            piece, piece, pass_sem.at[k], ar_sem.at[i],
             device_id={"hosts": lax.rem(me + k, n)}, device_id_type=MESH,
         )
 
-    def arrived(p):
-        piece = anchor.at[p // 2, p % 2]
-        pltpu.make_async_copy(piece, piece, ar_sem.at[p]).wait()
-
-    def when_not_root(k, act):
+    def arrived(i):
+        host, start, count = pieces[i]
+        piece = anchor.at[pl.ds(start, count)]
+        pltpu.make_async_copy(piece, piece, ar_sem.at[i]).wait()
+
+    def when_not_root(i, k, act):
         @pl.when(lax.rem(me + k, n) > 0)
         def _():
-            act(pass_on(k))
+            act(pass_on(i, k))
 
     @pl.when(is_root)
     def _():
         for c in range(kv):
             for copy in load_kv(c, anchor, anc_sem):
                 copy.wait()
-        for p in reversed(range(1, pieces)):
-            scatter(p).start()
-        each(n, lambda k: pass_on(k).start())
+        for i in reversed(range(owners)):
+            scatter(i).start()
 
     def q_copy(k):
         return pltpu.make_async_remote_copy(
@@ -130,12 +138,12 @@
 
     each(n, lambda k: q_copy(k).start())
 
-    is_owner = (lax.rem(me, spread) == 0) & (me > 0)
-
-    @pl.when(is_owner)
-    def _():
-        arrived(mine)
-        each(n, lambda k: when_not_root(k, lambda copy: copy.start()))
+    for i in range(owners):
+
+        @pl.when(me == pieces[i][0])
+        def _():
+            arrived(i)
+            each(n, lambda k: when_not_root(i, k, lambda copy: copy.start()))
 
     docs = jnp.broadcast_to(docs_ref[...].astype(jnp.float32), (block, block))
     at_row = lax.broadcasted_iota(jnp.int32, (block, block), 0)
@@ -167,28 +175,32 @@
     spans = tokens[:, heads:heads + 8] * SPAN_BASE + tokens[:, heads + 8:heads + 16]
     place = lax.broadcasted_iota(jnp.int32, (n, 8, block), 2) + me * block
     seen = (place.astype(jnp.float32) >= spans).reshape(n * group, block)
-    lane = lax.broadcasted_iota(jnp.int32, (n, group, HEAD_SIZE), 2) // 16
+    lane = lax.broadcasted_iota(jnp.int32, (n, group, HEAD_SIZE), 2) // 8
     stats = jnp.zeros((n, group, HEAD_SIZE), jnp.float32)
     ones = jnp.ones((block, HEAD_SIZE), jnp.bfloat16)
     for c in range(kv):
         part = tokens[:, c * group:(c + 1) * group].reshape(n * group, HEAD_SIZE)
         scores = lax.dot_general(
-            part.astype(jnp.bfloat16), own[c, 0], (((1,), (1,)), ((), ())),
+            part.astype(jnp.bfloat16), own[2 * c * block:(2 * c + 1) * block], (((1,), (1,)), ((), ())),
             preferred_element_type=jnp.float32,
         )
         scores = jnp.where(seen, scores, MASKED_SCORE)
-        peak = jnp.max(scores, -1, keepdims=True)
+        peak = jnp.max(scores, -1, keepdims=True).astype(jnp.bfloat16).astype(jnp.float32)
         weights = jnp.where(seen, jnp.exp2((scores - peak) * factor), 0.0)
         acc = jnp.dot(
-            weights.astype(jnp.bfloat16), jnp.concatenate([own[c, 1], ones], 1),
+            weights.astype(jnp.bfloat16), jnp.concatenate([own[(2 * c + 1) * block:2 * (c + 1) * block], ones], 1),
             preferred_element_type=jnp.float32,
         )
-        psend[:, c * group:(c + 1) * group, :] = acc[:, :HEAD_SIZE].reshape(n, group, HEAD_SIZE)
+        pwide[:, c * group:(c + 1) * group, :] = acc[:, :HEAD_SIZE].reshape(n, group, HEAD_SIZE)
         total = acc[:, HEAD_SIZE:].reshape(n, group, HEAD_SIZE)
-        stats = jnp.where(lane == 2 * c, total, stats)
+        coarse = total.astype(jnp.bfloat16).astype(jnp.float32)
+        stats = jnp.where(lane == 3 * c, coarse, stats)
+        stats = jnp.where(lane == 3 * c + 1, total - coarse, stats)
         peak = jnp.broadcast_to(peak, (n * group, HEAD_SIZE)).reshape(n, group, HEAD_SIZE)
-        stats = jnp.where(lane == 2 * c + 1, peak, stats)
-    psend[:, heads:heads + group, :] = stats
+        stats = jnp.where(lane == 3 * c + 2, peak, stats)
+    pwide[:, heads:heads + group, :] = stats
+    pwide[:, heads + group:, :] = jnp.zeros_like(stats)
+    psend[...] = pwide[...].astype(jnp.bfloat16)
     each(n, lambda k: p_copy(k).start())
     precv[me] = psend[me]
 
@@ -206,15 +218,16 @@
 
     @pl.loop(0, kv)
     def _(j):
-        c = lax.rem(mine // 2 + j, kv)
-        for i in range(2):
-
-            @pl.when((me > 0) & ~(is_owner & (2 * c + i == mine)))
+        c = j
+        for i in range(owners):
+
+            @pl.when((j == pieces[i][1] // (2 * block)) & (me > 0) & (me != pieces[i][0]))
             def _():
-                arrived(2 * c + i)
-
-        keys = jnp.concatenate([anchor[c, 0], own[c, 0]], 0)
-        values = jnp.concatenate([anchor[c, 1], own[c, 1]], 0)
+                arrived(i)
+
+        at = pl.multiple_of(2 * c * block, block)
+        keys = jnp.concatenate([anchor[pl.ds(at, block)], own[pl.ds(at, block)]], 0)
+        values = jnp.concatenate([anchor[pl.ds(at + block, block)], own[pl.ds(at + block, block)]], 0)
         values = jnp.concatenate([values, wide_ones], 1)
         for g in range(0, group, 2):
             queries = jnp.concatenate(
@@ -240,13 +253,14 @@
         pltpu.make_async_copy(precv.at[source], precv.at[source], pr_sem.at[source]).wait()
 
     each(n, p_arrived)
-    stats = precv[:, heads:heads + group, :]
-    for c in range(kv):
-        total = stats[:, :, 32 * c:32 * c + 1]
-        peak = stats[:, :, 32 * c + 16:32 * c + 17]
+    partials = precv[...].astype(jnp.float32)
+    stats = partials[:, heads:heads + group]
+    for c in range(kv):
+        total = stats[:, :, 24 * c:24 * c + 1] + stats[:, :, 24 * c + 8:24 * c + 9]
+        peak = stats[:, :, 24 * c + 16:24 * c + 17]
         scale = jnp.exp2((peak - jnp.max(peak, 0, keepdims=True)) * factor)
         total = jnp.sum(scale * total, 0)
-        merged = jnp.sum(scale * precv[:, c * group:(c + 1) * group, :], 0)
+        merged = jnp.sum(scale * partials[:, c * group:(c + 1) * group], 0)
         answer_ref[c * group:(c + 1) * group, :] = merged / total
 
     each(n, lambda k: q_copy(k).wait_send())
@@ -254,13 +268,14 @@
 
     @pl.when(is_root)
     def _():
-        for p in range(1, pieces):
-            scatter(p).wait_send()
-        each(n, lambda k: pass_on(k).wait_send())
-
-    @pl.when(is_owner)
-    def _():
-        each(n, lambda k: when_not_root(k, lambda copy: copy.wait_send()))
+        for i in range(owners):
+            scatter(i).wait_send()
+
+    for i in range(owners):
+
+        @pl.when(me == pieces[i][0])
+        def _():
+            each(n, lambda k: when_not_root(i, k, lambda copy: copy.wait_send()))
 
     for c in range(kv):
         put(c).wait()
@@ -289,16 +304,17 @@
             pltpu.VMEM(query_token_rows.shape, jnp.bfloat16),
             pltpu.VMEM((kv, block, width), jnp.bfloat16),
             pltpu.VMEM((kv, block, width), jnp.bfloat16),
-            pltpu.VMEM((kv, 2, block, HEAD_SIZE), jnp.bfloat16),
-            pltpu.VMEM((kv, 2, block, HEAD_SIZE), jnp.bfloat16),
+            pltpu.VMEM((2 * kv * block, HEAD_SIZE), jnp.bfloat16),
+            pltpu.VMEM((2 * kv * block, HEAD_SIZE), jnp.bfloat16),
             pltpu.VMEM((block, block), jnp.float32),
             pltpu.VMEM((heads + 16, HEAD_SIZE), jnp.float32),
             pltpu.VMEM((n, heads + 16, HEAD_SIZE), jnp.bfloat16),
-            pltpu.VMEM((n, heads + 8, HEAD_SIZE), jnp.float32),
-            pltpu.VMEM((n, heads + 8, HEAD_SIZE), jnp.float32),
+            pltpu.VMEM((n, heads + 16, HEAD_SIZE), jnp.float32),
+            pltpu.VMEM((n, heads + 16, HEAD_SIZE), jnp.bfloat16),
+            pltpu.VMEM((n, heads + 16, HEAD_SIZE), jnp.bfloat16),
             dma((kv, 3)), dma((kv, 2)), dma((kv,)), dma((2,)),
             dma((n,)), dma((n,)), dma((n,)), dma((n,)),
-            dma((2 * kv,)), dma((n,)), dma((2 * kv,)),
+            dma((7,)), dma((n,)), dma((7,)),
         ],
         compiler_params=pltpu.CompilerParams(
             collective_id=0, has_side_effects=True, vmem_limit_bytes=40 * 1024 * 1024

time: 29.3 us -> 25.4 us (0.87)
  Pallas kernels: 26.2 us -> 22.3 us
    pallas_call x1, Pallas kernels: 26.2 us -> 22.3 us  [on_device(): pl.pallas_call(functools.partial(kernel, n, kv, group, block), out_shape=...]
where the time goes in v4:
time: 25.4 us; the launch traced here: 25.2 us
  Pallas kernels  22.3 us (88%)
  local copies, waits for them, and re-layouts  1.59 us (6%)
  between operations  1.29 us (5%)
    pallas_call x1, Pallas kernels, on_device(): pl.pallas_call(functools.partial(kernel, n, kv, group, block), out_shape=...  22.3 us
    unnamed x2, local copies, waits for them, and re-layouts  1.59 us

profile of v4, /device:TPU:0, one launch (start us, length us, event | category | flops | bytes accessed | tf_op | source)
XLA Modules:
  0.0 25.2 jit_solution(7480647400769521352)
XLA Ops:
  1.3 22.3 %shard_map.77 = (bf16[128,4096]{1,0:T(8,128)(2,1)S(1)}, f32[32,128]{1,0:T(8,128)S(1)}) custom-call(bf16[128,4096]{1,0:T(8,128)(2,1)} %q_hbm.1, bf16[128,512]{1,0:T(8,128)(2,1)} %k_hbm.1, bf16[128,512]{1,0:T(8,128)(2,1)} %v_hbm.1, s32[1,128]{1,0:T(1,128)} %bitcast.8, bf16[1,4096]{1,0:T(2,128)(2,1)} %rows_hbm.1, s32[1]{0:T(128)S(6)} %copy.12.span_ref), custom_call_target="tpu_custom_call" | custom-call | tf_op jit(solution)/shard_map/pallas_call | solution.py:294
  23.6 0.6 %copy.10 = bf16[1,1,32,128]{3,1,2,0:T(2,128)(2,1)} copy(bf16[1,1,32,128]{3,2,1,0:T(8,128)(2,1)S(1)} %convert_bitcast_fusion) | data formatting | bytes 16384
  24.3 1.0 %copy.13 = bf16[128,4096]{1,0:T(8,128)(2,1)} copy(bf16[128,4096]{1,0:T(8,128)(2,1)S(1)} %get-tuple-element.8) | data formatting | bytes 2097152
  (1 shorter events, 0.0 us)

commit v5 on v4

--- a/solution.py
+++ b/solution.py
@@ -26,7 +26,7 @@
     n, kv, group, block,
     q_hbm, k_hbm, v_hbm, docs_hbm, rows_hbm, span_ref,
     out_hbm, answer_ref,
-    docs_ref, rows_ref, qbuf, obuf, own, anchor, bias, qrow, qall, pwide, psend, precv,
+    docs_ref, rows_ref, qbuf, obuf, own, anchor, bias, qrow, qall, psend, precv,
     in_sem, anc_sem, out_sem, small_sem, qs_sem, qr_sem, ps_sem, pr_sem, scatter_sem, pass_sem, ar_sem,
 ):
     me = lax.axis_index("hosts")
@@ -175,7 +175,7 @@
     spans = tokens[:, heads:heads + 8] * SPAN_BASE + tokens[:, heads + 8:heads + 16]
     place = lax.broadcasted_iota(jnp.int32, (n, 8, block), 2) + me * block
     seen = (place.astype(jnp.float32) >= spans).reshape(n * group, block)
-    lane = lax.broadcasted_iota(jnp.int32, (n, group, HEAD_SIZE), 2) // 8
+    lane = lax.broadcasted_iota(jnp.int32, (n, group, HEAD_SIZE), 2) // 16
     stats = jnp.zeros((n, group, HEAD_SIZE), jnp.float32)
     ones = jnp.ones((block, HEAD_SIZE), jnp.bfloat16)
     for c in range(kv):
@@ -185,22 +185,18 @@
             preferred_element_type=jnp.float32,
         )
         scores = jnp.where(seen, scores, MASKED_SCORE)
-        peak = jnp.max(scores, -1, keepdims=True).astype(jnp.bfloat16).astype(jnp.float32)
+        peak = jnp.max(scores, -1, keepdims=True)
         weights = jnp.where(seen, jnp.exp2((scores - peak) * factor), 0.0)
         acc = jnp.dot(
             weights.astype(jnp.bfloat16), jnp.concatenate([own[(2 * c + 1) * block:2 * (c + 1) * block], ones], 1),
             preferred_element_type=jnp.float32,
         )
-        pwide[:, c * group:(c + 1) * group, :] = acc[:, :HEAD_SIZE].reshape(n, group, HEAD_SIZE)
+        psend[:, c * group:(c + 1) * group, :] = acc[:, :HEAD_SIZE].reshape(n, group, HEAD_SIZE)
         total = acc[:, HEAD_SIZE:].reshape(n, group, HEAD_SIZE)
-        coarse = total.astype(jnp.bfloat16).astype(jnp.float32)
-        stats = jnp.where(lane == 3 * c, coarse, stats)
-        stats = jnp.where(lane == 3 * c + 1, total - coarse, stats)
+        stats = jnp.where(lane == 2 * c, total, stats)
         peak = jnp.broadcast_to(peak, (n * group, HEAD_SIZE)).reshape(n, group, HEAD_SIZE)
-        stats = jnp.where(lane == 3 * c + 2, peak, stats)
-    pwide[:, heads:heads + group, :] = stats
-    pwide[:, heads + group:, :] = jnp.zeros_like(stats)
-    psend[...] = pwide[...].astype(jnp.bfloat16)
+        stats = jnp.where(lane == 2 * c + 1, peak, stats)
+    psend[:, heads:heads + group, :] = stats
     each(n, lambda k: p_copy(k).start())
     precv[me] = psend[me]
 
@@ -253,11 +249,11 @@
         pltpu.make_async_copy(precv.at[source], precv.at[source], pr_sem.at[source]).wait()
 
     each(n, p_arrived)
-    partials = precv[...].astype(jnp.float32)
+    partials = precv[...]
     stats = partials[:, heads:heads + group]
     for c in range(kv):
-        total = stats[:, :, 24 * c:24 * c + 1] + stats[:, :, 24 * c + 8:24 * c + 9]
-        peak = stats[:, :, 24 * c + 16:24 * c + 17]
+        total = stats[:, :, 32 * c:32 * c + 1]
+        peak = stats[:, :, 32 * c + 16:32 * c + 17]
         scale = jnp.exp2((peak - jnp.max(peak, 0, keepdims=True)) * factor)
         total = jnp.sum(scale * total, 0)
         merged = jnp.sum(scale * partials[:, c * group:(c + 1) * group], 0)
@@ -309,9 +305,8 @@
             pltpu.VMEM((block, block), jnp.float32),
             pltpu.VMEM((heads + 16, HEAD_SIZE), jnp.float32),
             pltpu.VMEM((n, heads + 16, HEAD_SIZE), jnp.bfloat16),
-            pltpu.VMEM((n, heads + 16, HEAD_SIZE), jnp.float32),
-            pltpu.VMEM((n, heads + 16, HEAD_SIZE), jnp.bfloat16),
-            pltpu.VMEM((n, heads + 16, HEAD_SIZE), jnp.bfloat16),
+            pltpu.VMEM((n, heads + 8, HEAD_SIZE), jnp.float32),
+            pltpu.VMEM((n, heads + 8, HEAD_SIZE), jnp.float32),
             dma((kv, 3)), dma((kv, 2)), dma((kv,)), dma((2,)),
             dma((n,)), dma((n,)), dma((n,)), dma((n,)),
             dma((7,)), dma((n,)), dma((7,)),

time: 25.4 us -> 25.7 us (1.012)
  Pallas kernels: 22.3 us -> 22.6 us
    pallas_call x1, Pallas kernels: 22.3 us -> 22.6 us  [on_device(): pl.pallas_call(functools.partial(kernel, n, kv, group, block), out_shape=...]
where the time goes in v5:
time: 25.7 us; the launch traced here: 25.5 us
  Pallas kernels  22.6 us (88%)
  local copies, waits for them, and re-layouts  1.59 us (6%)
  between operations  1.29 us (5%)
    pallas_call x1, Pallas kernels, on_device(): pl.pallas_call(functools.partial(kernel, n, kv, group, block), out_shape=...  22.6 us
    unnamed x2, local copies, waits for them, and re-layouts  1.59 us

profile of v5, /device:TPU:0, one launch (start us, length us, event | category | flops | bytes accessed | tf_op | source)
XLA Modules:
  0.0 25.5 jit_solution(6178151484010429995)
XLA Ops:
  1.3 22.6 %shard_map.77 = (bf16[128,4096]{1,0:T(8,128)(2,1)S(1)}, f32[32,128]{1,0:T(8,128)S(1)}) custom-call(bf16[128,4096]{1,0:T(8,128)(2,1)} %q_hbm.1, bf16[128,512]{1,0:T(8,128)(2,1)} %k_hbm.1, bf16[128,512]{1,0:T(8,128)(2,1)} %v_hbm.1, s32[1,128]{1,0:T(1,128)} %bitcast.8, bf16[1,4096]{1,0:T(2,128)(2,1)} %rows_hbm.1, s32[1]{0:T(128)S(6)} %copy.12.span_ref), custom_call_target="tpu_custom_call" | custom-call | tf_op jit(solution)/shard_map/pallas_call | solution.py:290
  23.9 0.6 %copy.10 = bf16[1,1,32,128]{3,1,2,0:T(2,128)(2,1)} copy(bf16[1,1,32,128]{3,2,1,0:T(8,128)(2,1)S(1)} %convert_bitcast_fusion) | data formatting | bytes 16384
  24.5 1.0 %copy.13 = bf16[128,4096]{1,0:T(8,128)(2,1)} copy(bf16[128,4096]{1,0:T(8,128)(2,1)S(1)} %get-tuple-element.8) | data formatting | bytes 2097152
  (1 shorter events, 0.0 us)
